TPU v7x, 128 devices: a whole 4x4x4 slice. The times are simulated.
128 devices in a mesh: dp: 4 (over y), seq: 32 (over z, x, core).
Axes of the slice: x: 4, y: 4, z: 4, core: 2. Of those that a mesh axis runs over, the one named last changes fastest.
Arguments:
- query: bfloat16 [16384, 3072], P(('dp', 'seq')), parts along dimension 0, may hold values from -24 to 24
- key_in: bfloat16 [16384, 3072], P(('dp', 'seq')), parts along dimension 0, may hold values from -24 to 24
- value: bfloat16 [16384, 3072], P(('dp', 'seq')), parts along dimension 0, may hold values from -6 to 6
- grad_out: bfloat16 [16384, 3072], P(('dp', 'seq')), parts along dimension 0, may hold values from -6 to 6
- masks: int32 [96, 32, 32], P('dp'), parts along dimension 0, may hold values from 0 to 1, as said below
Outputs:
- attn_out: bfloat16 [16384, 3072], P(('dp', 'seq')), parts along dimension 0
- grad_query: bfloat16 [16384, 3072], P(('dp', 'seq')), parts along dimension 0
- grad_key: bfloat16 [16384, 3072], P(('dp', 'seq')), parts along dimension 0
- grad_value: bfloat16 [16384, 3072], P(('dp', 'seq')), parts along dimension 0
There are 4 independent parts, one for each index of `dp`. A program takes and returns all parts, laid end to end along the dimension named above; each array names one. Nothing has to cross between parts.
Inputs may be any that keep to these rules, and one draw needn't show every extreme that they name: masks[h, i, i] is 1 for every head h and block i.
All inputs are finite; a program needn't handle non-finite values.
Results may differ from a plain program's by a relative error of at most 0.012.
Values may be sent and summed in bfloat16 or wider, within the bound.
No kernel may reach another device: no remote copies, remote signals or barrier semaphores. Data moves between devices by JAX's collectives and lax.ppermute only.
A program may use at most 128 MiB of HBM per device.

v0:
```python
import math

import jax
import jax.numpy as jnp
from jax import lax
from jax.sharding import PartitionSpec as P


def for_sending(array):

    def short(part):
        return part.astype(jnp.bfloat16) if part.dtype == jnp.float32 else part

    return jax.tree.map(short, array)


def attend(q_rows, keys, values, grads, mask_rows, tile):
    rows_total, width = q_rows.shape
    key_count = keys.shape[0]
    key_blocks = key_count // tile
    block_rows = math.gcd(512, rows_total)
    scale = width ** (-0.5)

    def step(carry, index):
        key_acc, value_acc = carry
        start = index * block_rows
        q_block = lax.dynamic_slice_in_dim(q_rows, start, block_rows, 0)
        g_block = lax.dynamic_slice_in_dim(grads, start, block_rows, 0)
        m_block = lax.dynamic_slice_in_dim(
            mask_rows, index * (block_rows // tile), block_rows // tile, 0
        )
        scores = jnp.einsum("qd,kd->qk", q_block, keys, preferred_element_type=jnp.float32) * scale
        live = (m_block > 0)[:, None, :, None]
        shaped = scores.reshape(block_rows // tile, tile, key_blocks, tile)
        scores = jnp.where(live, shaped, -jnp.inf).reshape(block_rows, key_count)
        highest = jnp.max(scores, axis=1, keepdims=True)
        raised = jnp.exp(scores - highest)
        probs = raised / jnp.sum(raised, axis=1, keepdims=True)
        probs_low = probs.astype(jnp.bfloat16)
        out_rows = jnp.einsum("qk,kd->qd", probs_low, values, preferred_element_type=jnp.float32)
        delta = jnp.sum(g_block.astype(jnp.float32) * out_rows, axis=1, keepdims=True)
        grad_probs = jnp.einsum("qd,kd->qk", g_block, values, preferred_element_type=jnp.float32)
        grad_scores = (probs * (grad_probs - delta)).astype(jnp.bfloat16)
        query_grad = (
            scale * jnp.einsum("qk,kd->qd", grad_scores, keys, preferred_element_type=jnp.float32)
        ).astype(jnp.bfloat16)
        key_acc = key_acc + scale * jnp.einsum(
            "qk,qd->kd", grad_scores, q_block, preferred_element_type=jnp.float32
        )
        value_acc = value_acc + jnp.einsum(
            "qk,qd->kd", probs_low, g_block, preferred_element_type=jnp.float32
        )
        return ((key_acc, value_acc), (out_rows.astype(jnp.bfloat16), query_grad))

    empty = jnp.zeros((key_count, width), jnp.float32)
    (key_acc, value_acc), (outs, query_grads) = lax.scan(
        step, (empty, empty), jnp.arange(rows_total // block_rows)
    )
    return (
        outs.reshape(rows_total, width),
        query_grads.reshape(rows_total, width),
        key_acc.astype(jnp.bfloat16),
        value_acc.astype(jnp.bfloat16),
    )


def body(query, key_in, value, grad_out, masks):
    peers = lax.axis_size("seq")
    position = lax.axis_index("seq")
    tok_rows = query.shape[0]
    heads = masks.shape[0]
    blocks = masks.shape[1]
    width = query.shape[1] // heads
    seq_rows = tok_rows * peers
    half_rows = seq_rows // 2
    tile = seq_rows // blocks
    items = 2 * heads
    slots = items // peers + 1
    item_cost = jnp.sum(masks.reshape(heads, 2, blocks // 2, blocks), axis=(2, 3)).reshape(items)
    order = jnp.argsort(-item_cost, stable=True)
    ranks_all = jnp.arange(items, dtype=jnp.int32)
    lap = ranks_all // peers
    within = ranks_all % peers
    snake = jnp.where(lap % 2 == 0, within, peers - 1 - within)
    inverse = jnp.argsort(order, stable=True)
    plan = jnp.take(snake, inverse)
    item_ids = jnp.arange(items, dtype=jnp.int32)
    device_hot = (plan[:, None] == jnp.arange(peers, dtype=jnp.int32)[None, :]).astype(jnp.int32)
    before = jnp.cumsum(device_hot, axis=0) - device_hot
    rank = jnp.sum(before * device_hot, axis=1)
    rank_hot = (rank[:, None] == jnp.arange(slots, dtype=jnp.int32)[None, :]).astype(jnp.int32)
    slot_hot = (device_hot[:, :, None] * rank_hot[:, None, :]).reshape(items, peers * slots)
    slot_head = jnp.sum(slot_hot * (item_ids // 2)[:, None], axis=0)
    slot_half = jnp.sum(slot_hot * (item_ids % 2)[:, None], axis=0)
    slot_used = jnp.sum(slot_hot, axis=0)
    head_hot = (slot_head[:, None] == jnp.arange(heads, dtype=jnp.int32)[None, :]) & (
        slot_used[:, None] > 0
    )
    my_half = position // (peers // 2)
    own_hot = head_hot & (slot_half[:, None] == my_half)
    all_weights = head_hot.astype(jnp.bfloat16)
    own_weights = own_hot.astype(jnp.bfloat16)

    def pick(array):
        return jnp.take(array.reshape(tok_rows, heads, width), slot_head, axis=1)

    got_q, got_k, got_v, got_g = (
        lax.all_to_all(pick(query), "seq", split_axis=1, concat_axis=0, tiled=True),
        lax.all_to_all(pick(key_in), "seq", split_axis=1, concat_axis=0, tiled=True),
        lax.all_to_all(pick(value), "seq", split_axis=1, concat_axis=0, tiled=True),
        lax.all_to_all(pick(grad_out), "seq", split_axis=1, concat_axis=0, tiled=True),
    )

    def query_rows(slot, start):
        q_head = lax.dynamic_index_in_dim(got_q, slot, 1, keepdims=False)
        g_head = lax.dynamic_index_in_dim(got_g, slot, 1, keepdims=False)
        return (
            lax.dynamic_slice_in_dim(q_head, start, half_rows, 0),
            lax.dynamic_slice_in_dim(g_head, start, half_rows, 0),
        )

    my_heads = lax.dynamic_slice_in_dim(slot_head, position * slots, slots)
    my_halves = lax.dynamic_slice_in_dim(slot_half, position * slots, slots)

    def run_slot(slot):
        head = my_heads[slot]
        half = my_halves[slot]
        start = half * half_rows
        k_head = lax.dynamic_index_in_dim(got_k, slot, 1, keepdims=False)
        v_head = lax.dynamic_index_in_dim(got_v, slot, 1, keepdims=False)
        q_rows, g_rows = query_rows(slot, start)
        mask_head = lax.dynamic_index_in_dim(masks, head, 0, keepdims=False)
        mask_rows = lax.dynamic_slice_in_dim(
            mask_head, half * (half_rows // tile), half_rows // tile, 0
        )
        out_rows, query_grad, key_part, value_part = attend(
            q_rows, k_head, v_head, g_rows, mask_rows, tile
        )
        blank = jnp.zeros((seq_rows, width), jnp.bfloat16)
        out_full = lax.dynamic_update_slice_in_dim(blank, out_rows, start, 0)
        query_full = lax.dynamic_update_slice_in_dim(blank, query_grad, start, 0)
        return (out_full, query_full, key_part, value_part)

    results = lax.map(run_slot, jnp.arange(slots, dtype=jnp.int32))
    back_out, back_query, back_key, back_value = jax.tree.map(
        lambda part, own: part.astype(own.dtype),
        lax.all_to_all(for_sending(results), "seq", split_axis=1, concat_axis=0, tiled=True),
        results,
    )
    out_total = jnp.einsum("ktd,kh->thd", back_out, own_weights, preferred_element_type=jnp.float32)
    query_total = jnp.einsum(
        "ktd,kh->thd", back_query, own_weights, preferred_element_type=jnp.float32
    )
    key_total = jnp.einsum("ktd,kh->thd", back_key, all_weights, preferred_element_type=jnp.float32)
    value_total = jnp.einsum(
        "ktd,kh->thd", back_value, all_weights, preferred_element_type=jnp.float32
    )

    def finish(total):
        return total.astype(jnp.bfloat16).reshape(tok_rows, heads * width)

    return (finish(out_total), finish(query_total), finish(key_total), finish(value_total))


def solution(mesh):
    return jax.shard_map(
        body,
        mesh=mesh,
        in_specs=(
            P(("dp", "seq"), None),
            P(("dp", "seq"), None),
            P(("dp", "seq"), None),
            P(("dp", "seq"), None),
            P("dp", None, None),
        ),
        out_specs=(
            P(("dp", "seq"), None),
            P(("dp", "seq"), None),
            P(("dp", "seq"), None),
            P(("dp", "seq"), None),
        ),
        check_vma=False,
    )
```

profile of v0, /device:TPU:0, one launch (start us, length us, event | category | flops | bytes accessed | tf_op | source)
XLA Modules:
  0.0 607.3 jit_solution(17135824887501968035)
XLA Ops:
  21.6 4.2 select_bitcast_fusion
  25.8 36.6 %all_to_all.144 = bf16[128,64,128]{2,0,1:T(8,128)(2,1)S(1)} all-to-all(bf16[128,64,128]{2,0,1:T(8,128)(2,1)S(1)} %get-tuple-element.465), channel_id=1, replica_groups=mesh['dp'=4,'seq'=32] {'seq'}, dimensions={1} | all-to-all | bytes 4194304 | tf_op jit(solution)/shard_map/all_to_all | solution.py:108
  62.4 32.3 %all_to_all.145 = bf16[128,64,128]{2,0,1:T(8,128)(2,1)} all-to-all(bf16[128,64,128]{2,0,1:T(8,128)(2,1)S(1)} %get-tuple-element.463), channel_id=1, replica_groups=mesh['dp'=4,'seq'=32] {'seq'}, dimensions={1} | all-to-all | bytes 4194304 | tf_op jit(solution)/shard_map/all_to_all | solution.py:111
  94.7 32.3 %all_to_all.146 = bf16[128,64,128]{2,0,1:T(8,128)(2,1)} all-to-all(bf16[128,64,128]{2,0,1:T(8,128)(2,1)S(1)} %get-tuple-element.464), channel_id=1, replica_groups=mesh['dp'=4,'seq'=32] {'seq'}, dimensions={1} | all-to-all | bytes 4194304 | tf_op jit(solution)/shard_map/all_to_all | solution.py:109
  127.0 4.8 all-to-all-start.3
  137.0 24.7 %all-to-all-done.3 = bf16[128,64,128]{2,0,1:T(8,128)(2,1)} async-done(((bf16[128,64,128]{2,0,1:T(8,128)(2,1)}), bf16[128,64,128]{2,0,1:T(8,128)(2,1)}, u32[]{:S(2)}, u32[]{:S(2)}) %all-to-all-start.3) | async-done | bytes 2097184 | tf_op jit(solution)/shard_map/all_to_all | solution.py:110
  164.9 292.6 %while.61 = (s32[]{:T(128)}, bf16[2,4096,128]{2,1,0:T(8,128)(2,1)}, bf16[2,4096,128]{2,1,0:T(8,128)(2,1)}, bf16[2,4096,128]{2,1,0:T(8,128)(2,1)}, bf16[2,4096,12...) while((s32[]{:T(128)}, bf16[2,4096,128]{2,1,0:T(8,128)(2,1)}, ...), condition=%wide.region_15.17_spmd, body=%wide.region_9.16_spmd.sunk | while | flops 3250452992 | bytes 252074032 | solution.py:144
  188.4 119.7 %while.62 = (s32[]{:T(128)}, f32[4096,128]{1,0:T(8,128)}, f32[4096,128]{1,0:T(8,128)S(1)}, bf16[4,512,128]{2,1,0:T(8,128)(2,1)}, bf16[4,512,128]{2,1,0:T(8,128)(...) while((s32[]{:T(128)}, f32[4096,128]{1,0:T(8,128)}, ...), condition=%wide.region_14.15_spmd.clone, body=%wide.region_10.14_spmd.clone.sunk | while | flops 3249404416 | bytes 167133360 | solution.py:56
  204.6 5.0 fusion.82
  209.6 4.1 fusion.83
  234.0 5.7 fusion.82
  239.7 4.1 fusion.83
  264.1 5.7 fusion.82
  269.8 4.1 fusion.83
  294.2 5.7 fusion.82
  329.6 119.7 %while.62 = (s32[]{:T(128)}, f32[4096,128]{1,0:T(8,128)}, f32[4096,128]{1,0:T(8,128)S(1)}, bf16[4,512,128]{2,1,0:T(8,128)(2,1)}, bf16[4,512,128]{2,1,0:T(8,128)(...) while((s32[]{:T(128)}, f32[4096,128]{1,0:T(8,128)}, ...), condition=%wide.region_14.15_spmd.clone, body=%wide.region_10.14_spmd.clone.sunk | while | flops 3249404416 | bytes 167133360 | solution.py:56
  345.8 5.0 fusion.82
  375.2 5.7 fusion.82
  405.3 5.7 fusion.82
  411.0 4.1 fusion.83
  435.4 5.7 fusion.82
  457.5 5.8 copy.88
  467.3 5.8 copy.92
  473.1 24.2 %all-to-all-done.5 = bf16[2,4096,128]{2,0,1:T(2,128)(2,1)S(1)} async-done(((bf16[2,4096,128]{2,0,1:T(2,128)(2,1)}), bf16[2,4096,128]{2,0,1:T(2,128)(2,1)S(1)}, u32[]{:S(2)}, u32[]{:S(2)}) %all-to-all-start.5) | async-done | bytes 2097184 | tf_op jit(solution)/shard_map/all_to_all | solution.py:147
  497.3 4.8 all-to-all-start.7
  502.1 5.8 copy.90
  507.9 24.2 %all-to-all-done.7 = bf16[2,4096,128]{2,0,1:T(2,128)(2,1)} async-done(((bf16[2,4096,128]{2,0,1:T(2,128)(2,1)}), bf16[2,4096,128]{2,0,1:T(2,128)(2,1)}, u32[]{:S(2)}, u32[]{:S(2)}) %all-to-all-start.7) | async-done | bytes 2097184 | tf_op jit(solution)/shard_map/all_to_all | solution.py:147
  532.0 4.8 all-to-all-start.6
  536.8 5.8 copy.86
  542.6 24.2 %all-to-all-done.6 = bf16[2,4096,128]{2,0,1:T(2,128)(2,1)} async-done(((bf16[2,4096,128]{2,0,1:T(2,128)(2,1)}), bf16[2,4096,128]{2,0,1:T(2,128)(2,1)}, u32[]{:S(2)}, u32[]{:S(2)}) %all-to-all-start.6) | async-done | bytes 2097184 | tf_op jit(solution)/shard_map/all_to_all | solution.py:147
  566.8 4.8 all-to-all-start.4
  586.4 15.1 %all-to-all-done.4 = bf16[2,4096,128]{2,0,1:T(2,128)(2,1)} async-done(((bf16[2,4096,128]{2,0,1:T(2,128)(2,1)}), bf16[2,4096,128]{2,0,1:T(2,128)(2,1)}, u32[]{:S(2)}, u32[]{:S(2)}) %all-to-all-start.4) | async-done | bytes 2097184 | tf_op jit(solution)/shard_map/all_to_all | solution.py:147
  (363 shorter events, 253.8 us)
Async XLA Ops:
  0.6 10.0 %copy-start.17 = (bf16[128,3072]{1,0:T(8,128)(2,1)S(1)}, bf16[128,3072]{1,0:T(8,128)(2,1)}, u32[]{:S(2)}) copy-start(bf16[128,3072]{1,0:T(8,128)(2,1)} %param.14) | copy-start | bytes 2359300
  8.7 123.1 %copy-start.20 = (s32[64]{0:T(128)}, s32[64]{0:T(128)S(1)}, u32[]{:S(2)}) copy-start(s32[64]{0:T(128)S(1)} %eq.75) | copy-start | bytes 772
  127.0 34.7 %all-to-all-start.3 = ((bf16[128,64,128]{2,0,1:T(8,128)(2,1)}), bf16[128,64,128]{2,0,1:T(8,128)(2,1)}, u32[]{:S(2)}, u32[]{:S(2)}) async-start(bf16[128,64,128]{2,0,1:T(8,128)(2,1)} %get-tuple-element.462), calls=%async_computation.3 | async-start | bytes 4194304 | tf_op jit(solution)/shard_map/all_to_all | solution.py:110
  175.0 13.2 %copy-start.5 = (bf16[4096,2,128]{2,0,1:T(8,128)(2,1)}, bf16[4096,2,128]{2,0,1:T(8,128)(2,1)S(1)}, u32[]{:S(2)}) copy-start(bf16[4096,2,128]{2,0,1:T(8,128)(2,1)S(1)} %get-tuple-element.785) | copy-start | bytes 6291460 | tf_op jit(solution)/shard_map/while
  175.0 13.2 %copy-start.25 = (s32[2]{0:T(128)}, s32[2]{0:T(128)S(1)}, u32[]{:S(2)}) copy-start(s32[2]{0:T(128)S(1)} %get-tuple-element.783) | copy-start | bytes 28 | tf_op jit(solution)/shard_map/while
  175.0 13.2 %copy-start.27 = (s32[2]{0:T(128)}, s32[2]{0:T(128)S(1)}, u32[]{:S(2)}) copy-start(s32[2]{0:T(128)S(1)} %get-tuple-element.780) | copy-start | bytes 28 | tf_op jit(solution)/shard_map/while
  204.6 5.0 copy-start.4
  204.6 9.1 %copy-start.1 = (f32[512,4096]{1,0:T(8,128)S(1)}, f32[512,4096]{1,0:T(8,128)}, u32[]{:S(2)}) copy-start(f32[512,4096]{1,0:T(8,128)} %copy-done) | copy-start | bytes 25165828 | tf_op jit(solution)/shard_map/while/body/eval_jaxpr/while
  234.0 5.7 copy-start.4
  234.0 9.8 %copy-start.1 = (f32[512,4096]{1,0:T(8,128)S(1)}, f32[512,4096]{1,0:T(8,128)}, u32[]{:S(2)}) copy-start(f32[512,4096]{1,0:T(8,128)} %copy-done) | copy-start | bytes 25165828 | tf_op jit(solution)/shard_map/while/body/eval_jaxpr/while
  264.1 5.7 copy-start.4
  264.1 9.8 %copy-start.1 = (f32[512,4096]{1,0:T(8,128)S(1)}, f32[512,4096]{1,0:T(8,128)}, u32[]{:S(2)}) copy-start(f32[512,4096]{1,0:T(8,128)} %copy-done) | copy-start | bytes 25165828 | tf_op jit(solution)/shard_map/while/body/eval_jaxpr/while
  294.2 5.7 copy-start.4
  294.2 9.8 %copy-start.1 = (f32[512,4096]{1,0:T(8,128)S(1)}, f32[512,4096]{1,0:T(8,128)}, u32[]{:S(2)}) copy-start(f32[512,4096]{1,0:T(8,128)} %copy-done) | copy-start | bytes 25165828 | tf_op jit(solution)/shard_map/while/body/eval_jaxpr/while
  308.1 4.5 copy-start.15
  316.2 13.2 %copy-start.5 = (bf16[4096,2,128]{2,0,1:T(8,128)(2,1)}, bf16[4096,2,128]{2,0,1:T(8,128)(2,1)S(1)}, u32[]{:S(2)}) copy-start(bf16[4096,2,128]{2,0,1:T(8,128)(2,1)S(1)} %get-tuple-element.785) | copy-start | bytes 6291460 | tf_op jit(solution)/shard_map/while
  316.2 13.2 %copy-start.25 = (s32[2]{0:T(128)}, s32[2]{0:T(128)S(1)}, u32[]{:S(2)}) copy-start(s32[2]{0:T(128)S(1)} %get-tuple-element.783) | copy-start | bytes 28 | tf_op jit(solution)/shard_map/while
  316.2 13.2 %copy-start.27 = (s32[2]{0:T(128)}, s32[2]{0:T(128)S(1)}, u32[]{:S(2)}) copy-start(s32[2]{0:T(128)S(1)} %get-tuple-element.780) | copy-start | bytes 28 | tf_op jit(solution)/shard_map/while
  345.8 5.0 copy-start.4
  345.8 9.1 %copy-start.1 = (f32[512,4096]{1,0:T(8,128)S(1)}, f32[512,4096]{1,0:T(8,128)}, u32[]{:S(2)}) copy-start(f32[512,4096]{1,0:T(8,128)} %copy-done) | copy-start | bytes 25165828 | tf_op jit(solution)/shard_map/while/body/eval_jaxpr/while
  375.2 5.7 copy-start.4
  375.2 9.8 %copy-start.1 = (f32[512,4096]{1,0:T(8,128)S(1)}, f32[512,4096]{1,0:T(8,128)}, u32[]{:S(2)}) copy-start(f32[512,4096]{1,0:T(8,128)} %copy-done) | copy-start | bytes 25165828 | tf_op jit(solution)/shard_map/while/body/eval_jaxpr/while
  405.3 5.7 copy-start.4
  405.3 9.8 %copy-start.1 = (f32[512,4096]{1,0:T(8,128)S(1)}, f32[512,4096]{1,0:T(8,128)}, u32[]{:S(2)}) copy-start(f32[512,4096]{1,0:T(8,128)} %copy-done) | copy-start | bytes 25165828 | tf_op jit(solution)/shard_map/while/body/eval_jaxpr/while
  435.4 5.7 copy-start.4
  435.4 9.8 %copy-start.1 = (f32[512,4096]{1,0:T(8,128)S(1)}, f32[512,4096]{1,0:T(8,128)}, u32[]{:S(2)}) copy-start(f32[512,4096]{1,0:T(8,128)} %copy-done) | copy-start | bytes 25165828 | tf_op jit(solution)/shard_map/while/body/eval_jaxpr/while
  463.3 34.0 %all-to-all-start.5 = ((bf16[2,4096,128]{2,0,1:T(2,128)(2,1)}), bf16[2,4096,128]{2,0,1:T(2,128)(2,1)S(1)}, u32[]{:S(2)}, u32[]{:S(2)}) async-start(bf16[2,4096,128]{2,0,1:T(2,128)(2,1)} %copy.88), calls=%async_computation.5 | async-start | bytes 4194304 | tf_op jit(solution)/shard_map/all_to_all | solution.py:147
  497.3 34.7 %all-to-all-start.7 = ((bf16[2,4096,128]{2,0,1:T(2,128)(2,1)}), bf16[2,4096,128]{2,0,1:T(2,128)(2,1)}, u32[]{:S(2)}, u32[]{:S(2)}) async-start(bf16[2,4096,128]{2,0,1:T(2,128)(2,1)} %copy.92), calls=%async_computation.7 | async-start | bytes 4194304 | tf_op jit(solution)/shard_map/all_to_all | solution.py:147
  532.0 34.7 %all-to-all-start.6 = ((bf16[2,4096,128]{2,0,1:T(2,128)(2,1)}), bf16[2,4096,128]{2,0,1:T(2,128)(2,1)}, u32[]{:S(2)}, u32[]{:S(2)}) async-start(bf16[2,4096,128]{2,0,1:T(2,128)(2,1)} %copy.90), calls=%async_computation.6 | async-start | bytes 4194304 | tf_op jit(solution)/shard_map/all_to_all | solution.py:147
  542.6 29.0 %copy-start.22 = (s32[32,2]{0,1:T(2,128)S(1)}, s32[32,2]{0,1:T(2,128)}, u32[]{:S(2)}) copy-start(s32[32,2]{0,1:T(2,128)} %get-tuple-element.403) | copy-start | bytes 772
  542.6 29.2 %copy-start.24 = (s32[64]{0:T(128)S(1)}, s32[64]{0:T(128)}, u32[]{:S(2)}) copy-start(s32[64]{0:T(128)} %copy-done.23) | copy-start | bytes 772
  566.8 34.7 %all-to-all-start.4 = ((bf16[2,4096,128]{2,0,1:T(2,128)(2,1)}), bf16[2,4096,128]{2,0,1:T(2,128)(2,1)}, u32[]{:S(2)}, u32[]{:S(2)}) async-start(bf16[2,4096,128]{2,0,1:T(2,128)(2,1)} %copy.86), calls=%async_computation.4 | async-start | bytes 4194304 | tf_op jit(solution)/shard_map/all_to_all | solution.py:147
  (54 other events, 122.1 us)
where the time goes:
time: 616 us; the launch traced here: 607 us
  matrix products  173 us (28%)
  local copies, waits for them, and re-layouts  123 us (20%)
  waiting for transfers between devices  112 us (18%)
  blocking collectives  101 us (16%)
  other arithmetic  41.6 us (7%)
  loops' own time  31.7 us (5%)
  starting transfers between devices  23.1 us (4%)
    all_to_all x4, waiting for transfers between devices, body(): lax.all_to_all(for_sending(results), 'seq', split_axis=1, concat_axis=0,...  87.6 us
    dot_general x8, matrix products, step(): jnp.einsum('qk,qd->kd', grad_scores, q_block, preferred_element_type=jnp....  44 us
    all_to_all x1, blocking collectives, body(): lax.all_to_all(pick(query), 'seq', split_axis=1, concat_axis=0, tiled=True)  36.6 us
    dot_general x8, matrix products, step(): jnp.einsum('qk,kd->qd', grad_scores, keys, preferred_element_type=jnp.flo...  32.8 us
    all_to_all x1, blocking collectives, body(): lax.all_to_all(pick(key_in), 'seq', split_axis=1, concat_axis=0, tiled=True)  32.3 us
    all_to_all x1, blocking collectives, body(): lax.all_to_all(pick(grad_out), 'seq', split_axis=1, concat_axis=0, tiled=...  32.3 us
    dot_general x8, matrix products, step(): jnp.einsum('qd,kd->qk', g_block, values, preferred_element_type=jnp.float32)  29.9 us
    dot_general x8, matrix products, step(): jnp.einsum('qk,qd->kd', probs_low, g_block, preferred_element_type=jnp.fl...  26.3 us
  transfers between devices with their start and end apart: 5, of which 5 were waited for; matrix products, arithmetic and copies ran while one was open for 6% of the time, Pallas kernels for 0%

commit v1 on v0

v1 whole, which is shorter than its diff:
```python
import functools

import jax
import jax.numpy as jnp
from jax import lax
from jax.experimental import pallas as pl
from jax.experimental.pallas import tpu as pltpu
from jax.sharding import PartitionSpec as P

NT = (((1,), (1,)), ((), ()))
NN = (((1,), (0,)), ((), ()))
LOG2E = 1.4426950408889634


def dense_kernel(ck, split, bias_ref, own_ref, oth_ref, rows_ref, keep_ref, give_ref,
                 k_scr, v_scr, kt_scr, vt_scr, dk_scr, dv_scr, p0_scr, p1_scr, m_scr, qg_scr):
    half, slots, tile, width = own_ref.shape
    keys = 2 * half * tile
    lanes = 2 * tile
    tiles = bias_ref.shape[0]
    chunks = keys // ck
    sub = ck // tile
    scale = width ** -0.5
    c2 = scale * LOG2E
    ks = slots - 2
    f32, bf16 = jnp.float32, jnp.bfloat16
    per = 4 if split else 2
    hr = lanes // per

    def dot(a, b, dims=NN):
        return lax.dot_general(a, b, dims, preferred_element_type=f32)

    def prep(c, _):
        for src, base, s0 in ((own_ref, 0, ks), (oth_ref, half, 0)):
            k = src[c, s0]
            v = src[c, s0 + 1]
            at = pl.ds(pl.multiple_of((base + c) * tile, tile), tile)
            k_scr[at, :] = k
            v_scr[at, :] = v
            kt_scr[:, at] = k.T
            vt_scr[:, at] = v.T
            dk_scr[at, :] = jnp.zeros((tile, width), f32)
            dv_scr[at, :] = jnp.zeros((tile, width), f32)
        return 0

    lax.fori_loop(0, half, prep, 0)

    def q_tile(t):
        if split:
            return jnp.concatenate([own_ref[per * t + i, 0, :hr] for i in range(per)], 0)
        return jnp.concatenate([own_ref[per * t + i, 0] for i in range(per)], 0)

    def g_tile(t):
        if split:
            return jnp.concatenate([own_ref[per * t + i, 0, hr:] for i in range(per)], 0)
        return jnp.concatenate([own_ref[per * t + i, 1] for i in range(per)], 0)

    def put(t, slot, x):
        for i in range(per):
            part = x[i * hr:(i + 1) * hr].astype(bf16)
            if split:
                rows_ref[per * t + i, 0, slot * hr:(slot + 1) * hr] = part
            else:
                rows_ref[per * t + i, slot] = part

    def forward(t, c, p_ref, m_at, carry):
        m, l, o = carry
        at = pl.ds(pl.multiple_of(c * ck, ck), ck)
        s = dot(k_scr[at, :], q_tile(t), NT)
        bias = bias_ref[t, pl.ds(pl.multiple_of(c * sub, sub), sub), :]
        x = s.reshape(sub, tile, lanes) * c2 + bias[:, None, :]
        top = jnp.max(x.reshape(ck // 8, 8, lanes), axis=0)
        new = jnp.maximum(m, jnp.max(top, axis=0, keepdims=True))
        alpha = jnp.exp2(m - new)
        p = jnp.exp2(x.reshape(ck, lanes) - new)
        l = l * alpha + jnp.sum(jnp.sum(p.reshape(ck // 8, 8, lanes), axis=0), axis=0, keepdims=True)
        pb = p.astype(bf16)
        p_ref[at, :] = pb
        m_scr[m_at, pl.ds(c, 1), :] = new
        o = o * alpha + dot(vt_scr[:, at], pb)
        return new, l, o

    def start():
        return jnp.full((1, lanes), -1e30, f32), jnp.zeros((1, lanes), f32), jnp.zeros((width, lanes), f32)

    def close(t, m_at, carry):
        m, l, o = carry
        rl = 1.0 / l
        ot = o * rl
        put(t, 0, ot.T)
        delta = jnp.sum(g_tile(t).astype(f32).T * ot, axis=0, keepdims=True)
        m_scr[m_at, 0:chunks, :] = jnp.exp2(m_scr[m_at, 0:chunks, :] - m) * rl
        return delta

    def backward(t, c, p_ref, m_at, delta, dq):
        at = pl.ds(pl.multiple_of(c * ck, ck), ck)
        g = g_tile(t)
        q = q_tile(t)
        p = p_ref[at, :].astype(f32) * m_scr[m_at, pl.ds(c, 1), :]
        dp = dot(v_scr[at, :], g, NT)
        ds = (p * (dp - delta)).astype(bf16)
        dv_scr[at, :] += dot(p.astype(bf16), g)
        dk_scr[at, :] += dot(ds, q)
        return dq + dot(kt_scr[:, at], ds)

    zero_q = jnp.zeros((width, lanes), f32)
    refs = (p0_scr, p1_scr)

    first = lax.fori_loop(0, chunks, lambda c, x: forward(0, c, refs[0], 0, x), start())
    delta = close(0, 0, first)

    def both(t, cur, delta):
        def step(c, x):
            fwd, dq = x
            dq = backward(t - 1, c, refs[1 - cur], 1 - cur, delta, dq)
            fwd = forward(t, c, refs[cur], cur, fwd)
            return fwd, dq
        fwd, dq = lax.fori_loop(0, chunks, step, (start(), zero_q))
        put(t - 1, 1, (dq * scale).T)
        return close(t, cur, fwd)

    def pair(i, delta):
        delta = both(2 * i + 1, 1, delta)
        return both(2 * i + 2, 0, delta)

    delta = lax.fori_loop(0, tiles // 2 - 1, pair, delta)
    delta = both(tiles - 1, 1, delta)
    dq = lax.fori_loop(0, chunks, lambda c, x: backward(tiles - 1, c, refs[1], 1, delta, x), zero_q)
    put(tiles - 1, 1, (dq * scale).T)

    def finish(c, _):
        for base, ref in ((0, keep_ref), (half, give_ref)):
            at = pl.ds(pl.multiple_of((base + c) * tile, tile), tile)
            ref[c, 0] = (dk_scr[at, :] * scale).astype(bf16)
            ref[c, 1] = dv_scr[at, :].astype(bf16)
        return 0

    lax.fori_loop(0, half, finish, 0)


CHUNK = 2048


def attend_call(bias, own, oth, split, chunk=CHUNK):
    half, slots, tile, width = own.shape
    keys = 2 * half * tile
    rows = bias.shape[0] * bias.shape[2]
    f32, bf16 = jnp.float32, jnp.bfloat16
    vm = pl.BlockSpec(memory_space=pltpu.VMEM)
    return pl.pallas_call(
        functools.partial(dense_kernel, chunk, split),
        out_shape=(
            jax.ShapeDtypeStruct((half, slots - 2, tile, width), bf16),
            jax.ShapeDtypeStruct((half, 2, tile, width), bf16),
            jax.ShapeDtypeStruct((half, 2, tile, width), bf16),
        ),
        in_specs=[vm, vm, vm],
        out_specs=[vm, vm, vm],
        scratch_shapes=[
            pltpu.VMEM((keys, width), bf16),
            pltpu.VMEM((keys, width), bf16),
            pltpu.VMEM((width, keys), bf16),
            pltpu.VMEM((width, keys), bf16),
            pltpu.VMEM((keys, width), f32),
            pltpu.VMEM((keys, width), f32),
            pltpu.VMEM((keys, 2 * tile), bf16),
            pltpu.VMEM((keys, 2 * tile), bf16),
            pltpu.VMEM((2, 32, 2 * tile), f32),
            pltpu.VMEM((8, 128), f32),
        ],
        compiler_params=pltpu.CompilerParams(vmem_limit_bytes=40 * 2**20),
        cost_estimate=pl.CostEstimate(
            flops=12 * rows * keys * width, bytes_accessed=8 * keys * width * 2, transcendentals=rows * keys
        ),
    )(bias, own, oth)


def pack_kernel(chips, split, width, q_ref, k_ref, v_ref, g_ref, out_ref):
    rows = q_ref.shape[0]
    for i in range(chips):
        if split:
            part = i % 2
            at = slice(i // 2 * width, (i // 2 + 1) * width)
            cut = slice(part * (rows // 2), (part + 1) * (rows // 2))
            out_ref[i, 0, : rows // 2] = q_ref[cut, at]
            out_ref[i, 0, rows // 2 :] = g_ref[cut, at]
            out_ref[i, 1] = k_ref[:, at]
            out_ref[i, 2] = v_ref[:, at]
        else:
            at = slice(i * width, (i + 1) * width)
            out_ref[i, 0] = q_ref[:, at]
            out_ref[i, 1] = g_ref[:, at]
            out_ref[i, 2] = k_ref[:, at]
            out_ref[i, 3] = v_ref[:, at]


def pack_call(arrays, chips, split, width):
    rows, columns = arrays[0].shape
    whole = chips * width
    rest = columns - whole
    slots = 3 if split else 4
    if split:
        spec = pl.BlockSpec((rows, rest), lambda i: (0, whole // rest))
    else:
        spec = pl.BlockSpec((rows, whole), lambda i: (0, 0))
    return pl.pallas_call(
        functools.partial(pack_kernel, chips, split, width),
        grid=(1,),
        out_shape=jax.ShapeDtypeStruct((chips, slots, rows, width), jnp.bfloat16),
        in_specs=[spec] * 4,
        out_specs=pl.BlockSpec((chips, slots, rows, width), lambda i: (0, 0, 0, 0)),
        compiler_params=pltpu.CompilerParams(vmem_limit_bytes=24 * 2**20),
    )(*arrays)


def unpack_kernel(chips, width, a_ref, b_ref, out_ref, query_ref, key_ref, value_ref):
    rows = out_ref.shape[0]
    outs = (out_ref, query_ref, key_ref, value_ref)
    for i in range(chips):
        at = slice(i * width, (i + 1) * width)
        for s in range(4):
            outs[s][:, at] = a_ref[i, s]
    for i in range(chips // 2):
        at = slice((chips + i) * width, (chips + i + 1) * width)
        for s in range(2):
            cut = slice(s * (rows // 2), (s + 1) * (rows // 2))
            for part in range(2):
                outs[s][part * (rows // 2) : (part + 1) * (rows // 2), at] = b_ref[2 * i + part, 0, cut]
            one = b_ref[2 * i, 1 + s].astype(jnp.float32) + b_ref[2 * i + 1, 1 + s].astype(jnp.float32)
            outs[2 + s][:, at] = one.astype(jnp.bfloat16)


def unpack_call(back_a, back_b, heads):
    chips, _, rows, width = back_a.shape
    vm = pl.BlockSpec(memory_space=pltpu.VMEM)
    return pl.pallas_call(
        functools.partial(unpack_kernel, chips, width),
        out_shape=[jax.ShapeDtypeStruct((rows, heads * width), jnp.bfloat16)] * 4,
        in_specs=[vm, vm],
        out_specs=[vm] * 4,
        compiler_params=pltpu.CompilerParams(vmem_limit_bytes=24 * 2**20),
    )(back_a, back_b)


def body(query, key_in, value, grad_out, masks):
    peers = lax.axis_size("seq")
    chips = peers // 2
    position = lax.axis_index("seq")
    chip, core = position // 2, position % 2
    heads, blocks = masks.shape[:2]
    width = query.shape[1] // heads
    tile = query.shape[0]
    groups = [list(range(e, peers, 2)) for e in range(2)]
    swap = [(i, i ^ 1) for i in range(peers)]

    def exchange(array):
        return lax.all_to_all(array, "seq", 0, 0, axis_index_groups=groups, tiled=True)

    def bias_of(head, per):
        live = lax.dynamic_index_in_dim(masks, head, 0, keepdims=False).reshape(chips, 2, chips, 2)
        live = lax.dynamic_index_in_dim(live, core, 1, keepdims=False)
        live = jnp.where(core == 0, live, live[:, :, ::-1])
        live = live.transpose(0, 2, 1).reshape(chips // per, per, blocks).transpose(0, 2, 1)
        bias = jnp.where(live > 0, 0.0, -1e30).astype(jnp.float32)
        return jnp.repeat(bias, 2 * tile // per, axis=2)

    arrays = (query, key_in, value, grad_out)
    got_b = exchange(pack_call(arrays, chips, True, width))
    got_a = exchange(pack_call(arrays, chips, False, width))
    bias_b = bias_of(chips + chip // 2, 4)
    bias_a = bias_of(chip, 2)

    def run(got, bias, split):
        other = lax.ppermute(got[:, got.shape[1] - 2 :], "seq", swap)
        rows, keep, give = attend_call(bias, got, other, split)
        taken = lax.ppermute(give, "seq", swap)
        total = (keep.astype(jnp.float32) + taken.astype(jnp.float32)).astype(jnp.bfloat16)
        return exchange(jnp.concatenate([rows, total], axis=1))

    back_b = run(got_b, bias_b, True)
    back_a = run(got_a, bias_a, False)
    return tuple(unpack_call(back_a, back_b, heads))


def solution(mesh):
    tokens = P(("dp", "seq"), None)
    return jax.shard_map(
        body,
        mesh=mesh,
        in_specs=(tokens, tokens, tokens, tokens, P("dp", None, None)),
        out_specs=(tokens, tokens, tokens, tokens),
        check_vma=False,
    )
```

time: 616 us -> 209 us (0.34); the launches traced: 607 us -> 208 us
  matrix products: 173 us -> 0 us
  local copies, waits for them, and re-layouts: 123 us -> 14.6 us
  Pallas kernels: 0 us -> 71.9 us
  blocking collectives: 101 us -> 31.7 us
  waiting for transfers between devices: 112 us -> 68 us
  other arithmetic: 41.6 us -> 4.94 us
  loops' own time: 31.7 us -> 0 us
  starting transfers between devices: 23.1 us -> 16.4 us
    dot_general x52 -> x0, matrix products: 173 us -> none  [the longest x8 44 us: step(): jnp.einsum('qk,qd->kd', grad_scores, q_block, preferred_element_type=jnp....]
    pallas_call x0 -> x5, Pallas kernels: none -> 71.9 us  [the longest x2 66.2 us: attend_call(): pl.pallas_call(functools.partial(dense_kernel, chunk, split), out_shape=(...]
    all_to_all x3 -> x1, blocking collectives: 101 us -> 31.7 us  [exchange(): lax.all_to_all(array, 'seq', 0, 0, axis_index_groups=groups, tiled=True)]
    while x144 -> x0, local copies, waits for them, and re-layouts: 48.8 us -> none
    all_to_all x5 -> x3, waiting for transfers between devices: 112 us -> 68 us  [exchange(): lax.all_to_all(array, 'seq', 0, 0, axis_index_groups=groups, tiled=True)]
    another operation x3 -> x0, loops' own time: 31.7 us -> none  [the longest x1 21.1 us: body(): results = lax.map(run_slot, jnp.arange(slots, dtype=jnp.int32))]
    all_to_all x8 -> x0, local copies, waits for them, and re-layouts: 20.4 us -> none  [the longest x4 14.2 us: body(): lax.all_to_all(for_sending(results), 'seq', split_axis=1, concat_axis=0,...]
    dynamic_slice x24 -> x4, local copies, waits for them, and re-layouts: 18.7 us -> 1.06 us  [the longest x1 0.74 us: bias_of(): lax.dynamic_index_in_dim(masks, head, 0, keepdims=False)]
  transfers between devices with their start and end apart: 5 -> 7, of which waited for: 5 -> 3; matrix products, arithmetic and copies ran while one was open for 6% -> 5% of each run, Pallas kernels for 0% -> 33%
where the time goes in v1:
time: 209 us; the launch traced here: 208 us
  Pallas kernels  71.9 us (34%)
  waiting for transfers between devices  68 us (33%)
  blocking collectives  31.7 us (15%)
  starting transfers between devices  16.4 us (8%)
  local copies, waits for them, and re-layouts  14.6 us (7%)
  other arithmetic  4.94 us (2%)
    all_to_all x3, waiting for transfers between devices, exchange(): lax.all_to_all(array, 'seq', 0, 0, axis_index_groups=groups, tiled=True)  68 us
    pallas_call x2, Pallas kernels, attend_call(): pl.pallas_call(functools.partial(dense_kernel, chunk, split), out_shape=(...  66.2 us
    all_to_all x1, blocking collectives, exchange(): lax.all_to_all(array, 'seq', 0, 0, axis_index_groups=groups, tiled=True)  31.7 us
    all_to_all x3, starting transfers between devices, exchange(): lax.all_to_all(array, 'seq', 0, 0, axis_index_groups=groups, tiled=True)  15.6 us
    unnamed x20, local copies, waits for them, and re-layouts  8.43 us
  transfers between devices with their start and end apart: 7, of which 3 were waited for; matrix products, arithmetic and copies ran while one was open for 5% of the time, Pallas kernels for 33%

profile of v1, /device:TPU:0, one launch (start us, length us, event | category | flops | bytes accessed | tf_op | source)
XLA Modules:
  0.0 208.4 jit_solution(1056976299642870727)
XLA Ops:
  0.6 1.1 copy-done
  1.8 1.1 copy-done.2
  2.9 1.1 copy-done.4
  4.0 1.1 copy-done.6
  5.2 1.5 shard_map.86
  6.6 8.1 %all-to-all-start.2 = ((bf16[16,3,128,128]{3,2,1,0:T(8,128)(2,1)}), bf16[16,3,128,128]{3,2,1,0:T(8,128)(2,1)}, u32[]{:S(2)}, u32[]{:S(2)}) async-start(bf16[16,3,128,128]{3,2,1,0:T(8,128)(2,1)} %shard_map.86), calls=%async_computation.2 | async-start | bytes 3145728 | tf_op jit(solution)/shard_map/all_to_all | solution.py:257
  14.8 1.1 copy-done.3
  15.9 1.1 copy-done.5
  17.0 1.1 copy-done.7
  18.2 1.8 shard_map.84
  20.0 19.3 %all-to-all-done.2.own_ref = bf16[16,3,128,128]{3,2,1,0:T(8,128)(2,1)} async-done(((bf16[16,3,128,128]{3,2,1,0:T(8,128)(2,1)}), bf16[16,3,128,128]{3,2,1,0:T(8,128)(2,1)}, u32[]{:S(2)}, u32[]{:S(2)}) %all-to-all-start.2) | async-done | bytes 1572896 | tf_op jit(solution)/shard_map/all_to_all | solution.py:257
  39.3 3.7 %all-to-all-start = ((bf16[16,4,128,128]{3,2,1,0:T(8,128)(2,1)}), bf16[16,4,128,128]{3,2,1,0:T(8,128)(2,1)S(1)}, u32[]{:S(2)}, u32[]{:S(2)}) async-start(bf16[16,4,128,128]{3,2,1,0:T(8,128)(2,1)} %shard_map.84), calls=%async_computation | async-start | bytes 4194304 | tf_op jit(solution)/shard_map/all_to_all | solution.py:257
  43.0 2.3 %slice.9 = bf16[16,2,128,128]{3,2,1,0:T(8,128)(2,1)} slice(bf16[16,3,128,128]{3,2,1,0:T(8,128)(2,1)} %all-to-all-done.2.own_ref), slice={[0:16], [1:3], [0:128], [0:128]} | slice | bytes 2097152 | tf_op jit(solution)/shard_map/slice | solution.py:274
  45.4 0.7 constant_dynamic-slice_fusion.1
  46.6 26.4 %all-to-all-done.own_ref = bf16[16,4,128,128]{3,2,1,0:T(8,128)(2,1)S(1)} async-done(((bf16[16,4,128,128]{3,2,1,0:T(8,128)(2,1)}), bf16[16,4,128,128]{3,2,1,0:T(8,128)(2,1)S(1)}, u32[]{:S(2)}, u32[]{:S(2)}) %all-to-all-start) | async-done | bytes 2097184 | tf_op jit(solution)/shard_map/all_to_all | solution.py:257
  73.1 1.1 slice.8
  74.4 0.3 broadcast_in_dim.20
  74.7 0.2 reshape.35.bias_ref
  75.3 0.2 broadcast_in_dim.21
  75.5 0.2 reshape.37.bias_ref
  75.8 23.2 %shard_map.87 = (bf16[16,1,128,128]{3,2,1,0:T(8,128)(2,1)S(1)}, bf16[16,2,128,128]{3,2,1,0:T(8,128)(2,1)S(1)}, bf16[16,2,128,128]{3,2,1,0:T(8,128)(2,1)S(1)}) custom-call(f32[4,32,256]{2,1,0:T(8,128)S(1)} %reshape.37.bias_ref, bf16[16,3,128,128]{3,2,1,0:T(8,128)(2,1)} %all-to-all-done.2.own_ref, bf16[16,2,128,128]{3,2,1,0:T(8,128)(2,1)} %collective-permute-done.2.oth_ref), custom_call_target="tpu_custom_call" | custom-call | flops 6442450944 | bytes 8388608 | tf_op jit(solution)/shard_map/pallas_call | solution.py:150
  99.0 0.8 collective-permute-start.3
  99.8 43.0 %shard_map.85 = (bf16[16,2,128,128]{3,2,1,0:T(8,128)(2,1)S(1)}, bf16[16,2,128,128]{3,2,1,0:T(8,128)(2,1)S(1)}, bf16[16,2,128,128]{3,2,1,0:T(8,128)(2,1)}) custom-call(f32[8,32,256]{2,1,0:T(8,128)S(1)} %reshape.35.bias_ref, bf16[16,4,128,128]{3,2,1,0:T(8,128)(2,1)S(1)} %all-to-all-done.own_ref, bf16[16,2,128,128]{3,2,1,0:T(8,128)(2,1)} %collective-permute-done.oth_ref), custom_call_target="tpu_custom_call" | custom-call | flops 12884901888 | bytes 8388608 | tf_op jit(solution)/shard_map/pallas_call | solution.py:150
  142.8 0.5 add_convert_fusion
  143.3 0.5 copy-done.8
  143.8 1.3 pad_maximum_fusion.1
  145.1 3.7 %all-to-all-start.3 = ((bf16[16,3,128,128]{3,2,1,0:T(8,128)(2,1)}), bf16[16,3,128,128]{3,2,1,0:T(8,128)(2,1)S(1)}, u32[]{:S(2)}, u32[]{:S(2)}) async-start(bf16[16,3,128,128]{3,2,1,0:T(8,128)(2,1)} %pad_maximum_fusion.1), calls=%async_computation.3 | async-start | bytes 3145728 | tf_op jit(solution)/shard_map/all_to_all | solution.py:257
  148.8 1.7 add_convert_fusion.1
  150.5 1.5 pad_maximum_fusion
  152.0 22.3 %all-to-all-done.3.b_ref = bf16[16,3,128,128]{3,2,1,0:T(8,128)(2,1)S(1)} async-done(((bf16[16,3,128,128]{3,2,1,0:T(8,128)(2,1)}), bf16[16,3,128,128]{3,2,1,0:T(8,128)(2,1)S(1)}, u32[]{:S(2)}, u32[]{:S(2)}) %all-to-all-start.3) | async-done | bytes 1572896 | tf_op jit(solution)/shard_map/all_to_all | solution.py:257
  174.3 31.7 %all_to_all.20.a_ref = bf16[16,4,128,128]{3,2,1,0:T(8,128)(2,1)S(1)} all-to-all(bf16[16,4,128,128]{3,2,1,0:T(8,128)(2,1)} %pad_maximum_fusion), channel_id=1, replica_groups={{0,2,4,6,8,10,12,14,16,18,20,22,24,26,28,30},{1,3,5,7,9,11,13,15,17,19,..., dimensions={0} | all-to-all | bytes 4194304 | tf_op jit(solution)/shard_map/all_to_all | solution.py:257
  205.9 2.4 %shard_map.88 = (bf16[128,3072]{1,0:T(8,128)(2,1)}, bf16[128,3072]{1,0:T(8,128)(2,1)}, bf16[128,3072]{1,0:T(8,128)(2,1)}, bf16[128,3072]{1,0:T(8,128)(2,1)}) custom-call(bf16[16,4,128,128]{3,2,1,0:T(8,128)(2,1)S(1)} %all_to_all.20.a_ref, bf16[16,3,128,128]{3,2,1,0:T(8,128)(2,1)S(1)} %all-to-all-done.3.b_ref), custom_call_target="tpu_custom_call" | custom-call | tf_op jit(solution)/shard_map/pallas_call | solution.py:236
  (32 shorter events, 1.2 us)
Async XLA Ops:
  0.6 1.1 copy-start
  1.8 1.1 copy-start.2
  2.9 1.1 copy-start.4
  4.0 1.1 copy-start.6
  6.6 8.1 %copy-start.1 = (bf16[128,3072]{1,0:T(8,128)(2,1)S(1)}, bf16[128,3072]{1,0:T(8,128)(2,1)}, u32[]{:S(2)}) copy-start(bf16[128,3072]{1,0:T(8,128)(2,1)} %q_ref.3) | copy-start | bytes 2359300
  6.6 32.7 %all-to-all-start.2 = ((bf16[16,3,128,128]{3,2,1,0:T(8,128)(2,1)}), bf16[16,3,128,128]{3,2,1,0:T(8,128)(2,1)}, u32[]{:S(2)}, u32[]{:S(2)}) async-start(bf16[16,3,128,128]{3,2,1,0:T(8,128)(2,1)} %shard_map.86), calls=%async_computation.2 | async-start | bytes 3145728 | tf_op jit(solution)/shard_map/all_to_all | solution.py:257
  14.8 1.1 copy-start.3
  15.9 1.1 copy-start.5
  17.0 1.1 copy-start.7
  39.3 33.8 %all-to-all-start = ((bf16[16,4,128,128]{3,2,1,0:T(8,128)(2,1)}), bf16[16,4,128,128]{3,2,1,0:T(8,128)(2,1)S(1)}, u32[]{:S(2)}, u32[]{:S(2)}) async-start(bf16[16,4,128,128]{3,2,1,0:T(8,128)(2,1)} %shard_map.84), calls=%async_computation | async-start | bytes 4194304 | tf_op jit(solution)/shard_map/all_to_all | solution.py:257
  45.4 30.4 %collective-permute-start.2 = (bf16[16,2,128,128]{3,2,1,0:T(8,128)(2,1)}, bf16[16,2,128,128]{3,2,1,0:T(8,128)(2,1)}, u32[]{:S(2)}, u32[]{:S(2)}) collective-permute-start(bf16[16,2,128,128]{3,2,1,0:T(8,128)(2,1)} %slice.9), channel_id=1, source_target_pairs={{0,1},{1,0},{2,3},{3,2},{4,5},{5,4},{6,7},{7,6},{8,9},{9,8},{10,11... | collective-permute-start | bytes 3145736 | tf_op jit(solution)/shard_map/ppermute | solution.py:274
  74.1 25.7 %collective-permute-start = (bf16[16,2,128,128]{3,2,1,0:T(8,128)(2,1)}, bf16[16,2,128,128]{3,2,1,0:T(8,128)(2,1)}, u32[]{:S(2)}, u32[]{:S(2)}) collective-permute-start(bf16[16,2,128,128]{3,2,1,0:T(8,128)(2,1)} %slice.8), channel_id=1, source_target_pairs={{0,1},{1,0},{2,3},{3,2},{4,5},{5,4},{6,7},{7,6},{8,9},{9,8},{10,11... | collective-permute-start | bytes 3145736 | tf_op jit(solution)/shard_map/ppermute | solution.py:274
  99.0 43.8 %collective-permute-start.3 = (bf16[16,2,128,128]{3,2,1,0:T(8,128)(2,1)S(1)}, bf16[16,2,128,128]{3,2,1,0:T(8,128)(2,1)S(1)}, u32[]{:S(2)}, u32[]{:S(2)}) collective-permute-start(bf16[16,2,128,128]{3,2,1,0:T(8,128)(2,1)S(1)} %get-tuple-element.15), channel_id=1, source_target_pairs={{0,1},{1,0},{2,3},{3,2},{4,5},{5,4},{6,7},{7,6},{8,9},{9,8},{10,11... | collective-permute-start | bytes 3145736 | tf_op jit(solution)/shard_map/ppermute | solution.py:276
  142.8 1.0 copy-start.8
  142.8 6.0 %collective-permute-start.1 = (bf16[16,2,128,128]{3,2,1,0:T(8,128)(2,1)}, bf16[16,2,128,128]{3,2,1,0:T(8,128)(2,1)}, u32[]{:S(2)}, u32[]{:S(2)}) collective-permute-start(bf16[16,2,128,128]{3,2,1,0:T(8,128)(2,1)} %get-tuple-element.12), channel_id=1, source_target_pairs={{0,1},{1,0},{2,3},{3,2},{4,5},{5,4},{6,7},{7,6},{8,9},{9,8},{10,11... | collective-permute-start | bytes 3145736 | tf_op jit(solution)/shard_map/ppermute | solution.py:276
  145.1 29.2 %all-to-all-start.3 = ((bf16[16,3,128,128]{3,2,1,0:T(8,128)(2,1)}), bf16[16,3,128,128]{3,2,1,0:T(8,128)(2,1)S(1)}, u32[]{:S(2)}, u32[]{:S(2)}) async-start(bf16[16,3,128,128]{3,2,1,0:T(8,128)(2,1)} %pad_maximum_fusion.1), calls=%async_computation.3 | async-start | bytes 3145728 | tf_op jit(solution)/shard_map/all_to_all | solution.py:257
  148.8 1.7 copy-start.9
